TPU v7x, 32 devices: a whole 2x2x4 slice. The times are simulated.
32 devices in a mesh: row: 4 (over y, core), col: 2 (over x), rep: 4 (over z).
Axes of the slice: x: 2, y: 2, z: 4, core: 2. Of those that a mesh axis runs over, the one named last changes fastest.
Arguments:
- features: float32 [256, 4096], P('rep', ('col', 'row')), may hold values from -6 to 6
- weight: float32 [256, 256], replicated, may hold values from -0.375 to 0.375
- cotangent: float32 [256, 4096], P('rep', ('row', 'col')), may hold values from -6 to 6
- tile_values: float32 [1280, 128, 128], P(('row', 'col')), may hold values from -0.078125 to 0.078125
- tile_row: int32 [1280], P(('row', 'col')), may hold values from 0 to 7
- tile_col: int32 [1280], P(('row', 'col')), may hold values from 0 to 15
- tile_kind: int32 [1280], P(('row', 'col')), may hold values from 0 to 159
- tile_count: int32 [8], P(('row', 'col')), may hold values from 40 to 160, as said below
Outputs:
- output: float32 [256, 4096], P('rep', ('row', 'col'))
- input_grad: float32 [256, 4096], P('rep', ('col', 'row'))
- weight_grad: float32 [256, 256], P('rep')
Inputs may be any that keep to these rules, and one draw needn't show every extreme that they name: `tile_count`: a block's slots at or after its count are not part of the adjacency; some block uses all 160 slots. `tile_row`: slots may repeat a tile position; their tiles add. `tile_kind`: an index into the 160 stored tiles of the same block.
All inputs are finite; a program needn't handle non-finite values.
Results may differ from a plain program's by a relative error of at most 0.0001.
Values sent between devices are 32-bit elements; how exact they have to be, the bound alone decides.
A program may use at most 128 MiB of HBM per device.

v0:
```python
import jax
import jax.numpy as jnp
from jax import lax
from jax.sharding import PartitionSpec as P


def tile_terms(source, values, from_tile, to_tile, tile_kinds, live_weight, dest_tiles, transposed):
    feat_width = source.shape[0]
    tile_edge = values.shape[1]
    tiled = source.reshape(feat_width, source.shape[1] // tile_edge, tile_edge)
    picked = jnp.take(tiled, from_tile, axis=1)
    chosen = jnp.take(values, tile_kinds, axis=0)
    if transposed:
        products = jnp.einsum("fga,gab->fgb", picked, chosen, precision=lax.Precision.HIGHEST)
    else:
        products = jnp.einsum("fgb,gab->fga", picked, chosen, precision=lax.Precision.HIGHEST)
    onehot = (to_tile[:, None] == jnp.arange(dest_tiles, dtype=jnp.int32)[None, :]).astype(
        jnp.float32
    )
    onehot = onehot * live_weight[:, None]
    spread = jnp.einsum("fgt,gd->fdt", products, onehot, precision=lax.Precision.HIGHEST)
    return spread.reshape(feat_width, dest_tiles * tile_edge)


def aggregate(source, values, from_tile, to_tile, tile_kinds, live_count, dest_tiles, transposed):
    slot_total = tile_kinds.shape[0]
    live_weight = (jnp.arange(slot_total, dtype=jnp.int32) < live_count).astype(jnp.float32)
    return tile_terms(
        source, values, from_tile, to_tile, tile_kinds, live_weight, dest_tiles, transposed
    )


def local(features, weight, cotangent, tile_values, tile_row, tile_col, tile_kind, tile_count):
    n_rowdev = lax.axis_size("row")
    n_coldev = lax.axis_size("col")
    n_repdev = lax.axis_size("rep")
    quarter = weight.shape[0] // n_repdev
    rep_index = lax.axis_index("rep")
    own_rows = lax.dynamic_slice_in_dim(weight, rep_index * quarter, quarter, 0)
    stretch_len = features.shape[1]
    tile_edge = tile_values.shape[1]
    live_count = tile_count[0]
    row_tiles = n_coldev * stretch_len // tile_edge
    col_tiles = n_rowdev * stretch_len // tile_edge
    mixed = lax.psum_scatter(
        lax.dot_general(
            own_rows,
            features,
            (((0,), (0,)), ((), ())),
            precision=lax.Precision.HIGHEST,
            preferred_element_type=jnp.float32,
        ),
        "rep",
        scatter_dimension=0,
        tiled=True,
    )
    column_block = lax.all_gather(mixed, "row", axis=1, tiled=True)
    partial_value = aggregate(
        column_block, tile_values, tile_col, tile_row, tile_kind, live_count, row_tiles, False
    )
    summed = lax.psum_scatter(partial_value, "col", scatter_dimension=1, tiled=True)
    output, pullback = jax.vjp(lambda v: jax.nn.gelu(v, approximate=True), summed)
    (grad_pre,) = pullback(cotangent)
    row_block = lax.all_gather(grad_pre, "col", axis=1, tiled=True)
    partial_back = aggregate(
        row_block, tile_values, tile_row, tile_col, tile_kind, live_count, col_tiles, True
    )
    grad_mixed = lax.psum_scatter(partial_back, "row", scatter_dimension=1, tiled=True)
    whole = lax.all_gather(grad_mixed, "rep", axis=0, tiled=True)
    input_grad = jnp.dot(
        own_rows, whole, preferred_element_type=jnp.float32, precision=lax.Precision.HIGHEST
    )
    weight_part = lax.dot_general(
        features,
        whole,
        (((1,), (1,)), ((), ())),
        precision=lax.Precision.HIGHEST,
        preferred_element_type=jnp.float32,
    )
    node_total = stretch_len * n_rowdev * n_coldev
    weight_grad = lax.psum(weight_part * float(node_total) ** (-0.5), ("row", "col"))
    return (output, input_grad, weight_grad)


def solution(mesh):
    return jax.shard_map(
        local,
        mesh=mesh,
        in_specs=(
            P("rep", ("col", "row")),
            P(),
            P("rep", ("row", "col")),
            P(("row", "col"), None, None),
            P(("row", "col")),
            P(("row", "col")),
            P(("row", "col")),
            P(("row", "col")),
        ),
        out_specs=(P("rep", ("row", "col")), P("rep", ("col", "row")), P("rep", None)),
        check_vma=False,
    )
```

profile of v0, /device:TPU:0, one launch (start us, length us, event | category | flops | bytes accessed | tf_op | source)
XLA Modules:
  0.0 217.2 jit_solution(3423354149670851976)
XLA Ops:
  7.2 0.0 copy-start
  7.2 0.0 reduce-scatter.4.cloned.1.call-start
  7.2 0.9 copy-done
  8.1 2.3 %fusion.39 = f32[256,512]{1,0:T(8,128)} fusion(f32[64,512]{1,0:T(8,128)} %param.10, f32[256,256]{1,0:T(8,128)S(1)} %copy-done, s32[]{:T(128)S(6)} %select_n.27), kind=kOutput, calls=%fused_computation.42 | convolution fusion | flops 100663296 | bytes 720900 | tf_op jit(solution)/shard_map/dot_general | solution.py:46
  10.5 0.0 reduce-scatter.4.cloned.1.call-update
  10.5 0.0 reduce-scatter.6.cloned.1.call-start
  11.2 0.7 compare_select_fusion
  11.9 0.0 copy-start.3
  11.9 0.0 copy-start.5
  11.9 14.2 %gather_fusion.2 = f32[160,128,128]{2,1,0:T(8,128)} fusion(f32[160,128,128]{2,1,0:T(8,128)} %param.13, s32[1024]{0:T(1024)S(1)} %pad_clamp_fusion.2), kind=kCustom, calls=%fused_computation.clone | custom fusion | bytes 20972160 | tf_op jit(solution)/shard_map/jit(_take)/gather | solution.py:12
  26.1 0.0 copy-done.3
  26.1 0.0 copy-done.5
  26.1 8.9 %reduce-scatter.4.cloned.1.call-done = f32[64,512]{1,0:T(8,128)} async-done(((f32[256,512]{1,0:T(8,128)}), f32[64,512]{1,0:T(8,128)}) %reduce-scatter.4.cloned.1.call-update) | async-done | bytes 131088 | tf_op jit(solution)/shard_map/reduce_scatter | solution.py:45
  35.0 7.3 %all_gather.9 = f32[64,2048]{1,0:T(8,128)S(1)} all-gather(f32[64,512]{1,0:T(8,128)} %reduce-scatter.4.cloned.1.call-done), channel_id=1, replica_groups=mesh['row'=4,'col'=2,'rep'=4] {'row'}, dimensions={1}, use_global_device_ids=true | all-gather | bytes 655360 | tf_op jit(solution)/shard_map/all_gather | solution.py:57
  42.4 3.3 %gather_fusion = f32[160,64,128]{2,1,0:T(8,128)} fusion(f32[64,16,128]{2,0,1:T(8,128)S(1)} %copy_bitcast_fusion.1, s32[1024]{0:T(1024)S(1)} %pad_clamp_fusion.1), kind=kCustom, calls=%fused_computation.1 | custom fusion | bytes 10486400 | tf_op jit(solution)/shard_map/jit(_take)/gather | solution.py:11
  45.6 0.0 copy-start.4
  45.6 24.3 %fusion.20 = f32[64,160,128]{2,0,1:T(8,128)S(1)} fusion(f32[160,64,128]{2,1,0:T(8,128)} %gather_fusion, pred[160]{0:T(512)(128)(4,1)S(1)} %get-tuple-element.7, f32[160,128,128]{2,1,0:T(8,128)} %gather_fusion.2, pred[160]{0:T(512)(128)(4,1)S(1)} %get-tuple-element.6), kind=kOutput, calls=%fused_computation.23 | convolution fusion | flops 2017198080 | bytes 20971840 | tf_op jit(solution)/shard_map/fgb,gab->fga/dot_general | solution.py:16
  69.9 0.0 copy-done.4
  69.9 0.0 copy-start.2
  70.0 5.4 %fusion.8 = f32[8,64,128]{2,0,1:T(8,128)S(1)} fusion(f32[64,160,128]{2,0,1:T(8,128)S(1)} %fusion.20, f32[160]{0:T(256)S(1)} %compare_convert_fusion, s32[160]{0:T(256)S(1)} %copy-done.4), kind=kOutput, calls=%fused_computation.11 | convolution fusion | flops 125831680 | bytes 5506304 | tf_op jit(solution)/shard_map/fgt,gd->fdt/dot_general | solution.py:21
  75.4 0.8 copy.29
  76.1 0.0 reduce-scatter.6.cloned.1.call-update
  76.2 0.0 reduce-scatter.8.cloned.1.call-start
  76.2 9.5 %reduce-scatter.6.cloned.1.call-done = f32[64,512]{1,0:T(8,128)} async-done(((f32[64,1024]{1,0:T(8,128)}), f32[64,512]{1,0:T(8,128)}) %reduce-scatter.6.cloned.1.call-update) | async-done | bytes 131088 | tf_op jit(solution)/shard_map/reduce_scatter | solution.py:61
  85.7 0.0 copy-done.2
  85.7 1.7 fusion.36
  87.4 5.9 %all_gather.10 = f32[64,1024]{1,0:T(8,128)S(1)} all-gather(f32[64,512]{1,0:T(8,128)S(1)} %get-tuple-element.4), channel_id=1, replica_groups=mesh['row'=4,'col'=2,'rep'=4] {'col'}, dimensions={1}, use_global_device_ids=true | all-gather | bytes 393216 | tf_op jit(solution)/shard_map/all_gather | solution.py:64
  93.3 3.3 %gather_fusion.1 = f32[160,64,128]{2,1,0:T(8,128)} fusion(f32[64,8,128]{2,0,1:T(8,128)S(1)} %copy_bitcast_fusion.3, s32[1024]{0:T(1024)S(1)} %pad_clamp_fusion), kind=kCustom, calls=%fused_computation.2 | custom fusion | bytes 10486400 | tf_op jit(solution)/shard_map/jit(_take)/gather | solution.py:11
  96.5 13.9 %fusion.25 = f32[64,160,128]{2,0,1:T(8,128)S(1)} fusion(f32[160,64,128]{2,1,0:T(8,128)} %gather_fusion.1, pred[160]{0:T(512)(128)(4,1)S(1)} %compare_and_fusion.1, f32[160,128,128]{2,1,0:T(8,128)} %gather_fusion.2, pred[160]{0:T(512)(128)(4,1)S(1)} %get-tuple-element.6), kind=kOutput, calls=%fused_computation.24 | convolution fusion | flops 2017198080 | bytes 20971840 | tf_op jit(solution)/shard_map/fga,gab->fgb/dot_general | solution.py:14
  110.4 0.0 copy-start.1
  110.4 5.4 %fusion.6 = f32[16,64,128]{2,0,1:T(8,128)S(1)} fusion(f32[64,160,128]{2,0,1:T(8,128)S(1)} %fusion.25, f32[160]{0:T(256)S(1)} %compare_convert_fusion, s32[160]{0:T(256)S(1)} %copy-done.3), kind=kOutput, calls=%fused_computation.9 | convolution fusion | flops 251663360 | bytes 5768448 | tf_op jit(solution)/shard_map/fgt,gd->fdt/dot_general | solution.py:21
  115.9 1.0 copy.28
  116.8 0.0 reduce-scatter.8.cloned.1.call-update
  116.9 0.0 all-reduce.2.cloned.1.call-start
  116.9 21.8 %reduce-scatter.8.cloned.1.call-done = f32[64,512]{1,0:T(8,128)} async-done(((f32[64,2048]{1,0:T(8,128)}), f32[64,512]{1,0:T(8,128)}) %reduce-scatter.8.cloned.1.call-update) | async-done | bytes 131088 | tf_op jit(solution)/shard_map/reduce_scatter | solution.py:68
  138.7 15.8 %all_gather.11 = f32[256,512]{1,0:T(8,128)S(1)} all-gather(f32[64,512]{1,0:T(8,128)} %reduce-scatter.8.cloned.1.call-done), channel_id=1, replica_groups=mesh['row'=4,'col'=2,'rep'=4] {'rep'}, dimensions={0}, use_global_device_ids=true | all-gather | bytes 655360 | tf_op jit(solution)/shard_map/all_gather | solution.py:69
  154.5 0.0 copy-done.1
  154.5 1.2 fusion.30
  155.8 0.0 all-reduce.2.cloned.1.call-update
  155.8 1.1 fusion.37
  156.9 52.3 %all-reduce.2.cloned.1.call-done = f32[64,256]{1,0:T(8,128)} async-done(((f32[64,256]{1,0:T(8,128)}), f32[64,256]{1,0:T(8,128)}) %all-reduce.2.cloned.1.call-update) | async-done | bytes 65552 | tf_op jit(solution)/shard_map/psum | solution.py:81
  209.2 1.5 copy.32
  (10 shorter events, 0.1 us)
Async XLA Ops:
  7.2 1.0 copy-start
  7.2 27.8 %reduce-scatter.4.cloned.1.call-start = ((), (), s32[]{:S(2)}) async-start(), calls=%async_computation.3 | async-start | bytes 655360 | tf_op jit(solution)/shard_map/reduce_scatter | solution.py:45
  10.5 75.2 %reduce-scatter.6.cloned.1.call-start = ((), (), s32[]{:S(2)}) async-start(), calls=%async_computation.4 | async-start | bytes 393216 | tf_op jit(solution)/shard_map/reduce_scatter | solution.py:61
  11.9 14.2 %copy-start.3 = (s32[160]{0:T(256)S(1)}, s32[160]{0:T(256)}, u32[]{:S(2)}) copy-start(s32[160]{0:T(256)} %param.15) | copy-start | bytes 1924
  11.9 14.2 %copy-start.5 = (s32[160]{0:T(256)S(1)}, s32[160]{0:T(256)}, u32[]{:S(2)}) copy-start(s32[160]{0:T(256)} %param.16) | copy-start | bytes 1924
  45.6 24.3 %copy-start.4 = (s32[160]{0:T(256)S(1)}, s32[160]{0:T(256)}, u32[]{:S(2)}) copy-start(s32[160]{0:T(256)} %param.14) | copy-start | bytes 1924
  69.9 15.8 %copy-start.2 = (f32[64,512]{1,0:T(8,128)S(1)}, f32[64,512]{1,0:T(8,128)}, u32[]{:S(2)}) copy-start(f32[64,512]{1,0:T(8,128)} %param.12) | copy-start | bytes 393220
  76.2 62.5 %reduce-scatter.8.cloned.1.call-start = ((), (), s32[]{:S(2)}) async-start(), calls=%async_computation.5 | async-start | bytes 655360 | tf_op jit(solution)/shard_map/reduce_scatter | solution.py:68
  110.4 44.1 %copy-start.1 = (f32[64,512]{1,0:T(8,128)S(1)}, f32[64,512]{1,0:T(8,128)}, u32[]{:S(2)}) copy-start(f32[64,512]{1,0:T(8,128)} %param.10) | copy-start | bytes 393220
  116.9 92.3 %all-reduce.2.cloned.1.call-start = ((), (), s32[]{:S(2)}) async-start(), calls=%async_computation.6 | async-start | bytes 131072 | tf_op jit(solution)/shard_map/psum | solution.py:81
Sparse Core Ops, SparseCore 0:
  10.6 24.3 reduce-scatter.3
  76.3 9.3 reduce-scatter.5
  117.0 21.6 reduce-scatter.7
  155.9 53.2 all-reduce.1
where the time goes:
time: 218 us; the launch traced here: 217 us
  waiting for transfers between devices  92.5 us (42%)
  matrix products  53.7 us (25%)
  blocking collectives  29 us (13%)
  local copies, waits for them, and re-layouts  24.9 us (11%)
  between operations  14.5 us (7%)
  other arithmetic  2.38 us (1%)
    psum x1, waiting for transfers between devices, local(): lax.psum(weight_part * float(node_total) ** (-0.5), ('row', 'col'))  52.3 us
    dot_general x1, matrix products, tile_terms(): jnp.einsum('fgb,gab->fga', picked, chosen, precision=lax.Precision.HIGHEST)  24.3 us
    reduce_scatter x1, waiting for transfers between devices, local(): lax.psum_scatter(partial_back, 'row', scatter_dimension=1, tiled=True)  21.8 us
    all_gather x1, blocking collectives, local(): whole = lax.all_gather(grad_mixed, 'rep', axis=0, tiled=True)  15.8 us
    gather x1, local copies, waits for them, and re-layouts, tile_terms(): chosen = jnp.take(values, tile_kinds, axis=0)  14.2 us
    dot_general x1, matrix products, tile_terms(): jnp.einsum('fga,gab->fgb', picked, chosen, precision=lax.Precision.HIGHEST)  13.9 us
    dot_general x2, matrix products, tile_terms(): jnp.einsum('fgt,gd->fdt', products, onehot, precision=lax.Precision.HIGHEST)  10.8 us
    reduce_scatter x1, waiting for transfers between devices, local(): lax.psum_scatter(partial_value, 'col', scatter_dimension=1, tiled=True)  9.45 us
  transfers between devices with their start and end apart: 4, of which 4 were waited for; matrix products, arithmetic and copies ran while one was open for 7% of the time, Pallas kernels for 0%

commit v1 on v0

--- a/solution.py
+++ b/solution.py
@@ -1,7 +1,381 @@
+import functools
+
 import jax
 import jax.numpy as jnp
 from jax import lax
+from jax.experimental import pallas as pl
+from jax.experimental.pallas import tpu as pltpu
 from jax.sharding import PartitionSpec as P
+
+MESH = pl.DeviceIdType.MESH
+F32, BF16 = jnp.float32, jnp.bfloat16
+DENSE_BYTES = 16 * 2**20
+NT = (((1,), (1,)), ((), ()))
+NN = (((1,), (0,)), ((), ()))
+
+
+def split(x):
+    high = x.astype(BF16)
+    return high, (x - high.astype(F32)).astype(BF16)
+
+
+def dot_split(stacked, high, b_high, b_low, dims):
+    rows = high.shape[0]
+    both = lax.dot_general(stacked, b_high, dims, preferred_element_type=F32)
+    cross = lax.dot_general(high, b_low, dims, preferred_element_type=F32)
+    return both[:rows] + both[rows:] + cross
+
+
+def product(a, b, dims):
+    a_high, a_low = split(a)
+    return dot_split(jnp.concatenate([a_high, a_low], 0), a_high, *split(b), dims)
+
+
+def dense_kernel(row_ref, col_ref, kind_ref, count_ref, values, high_ref, low_ref, held, total, sems):
+    step = pl.program_id(0)
+    edge = held.shape[1]
+    col_tiles = pl.num_programs(0) * (high_ref.shape[3] // edge)
+
+    @pl.when(step == 0)
+    def _():
+        parts = sems.shape[0]
+        size = held.shape[0] // parts
+        copies = [
+            pltpu.make_async_copy(
+                values.at[pl.ds(k * size, size)], held.at[pl.ds(k * size, size)], sems.at[k]
+            )
+            for k in range(parts)
+        ]
+        for copy in copies:
+            copy.start()
+
+        @pl.loop(0, total.shape[0])
+        def _(place):
+            total[place] = jnp.zeros(total.shape[1:], F32)
+
+        for copy in copies:
+            copy.wait()
+
+        def add(slot, carry):
+            place = row_ref[slot] * col_tiles + col_ref[slot]
+            total[place] = total[place] + held[kind_ref[slot]]
+            return carry
+
+        lax.fori_loop(0, count_ref[0], add, 0)
+
+    _, halves, rows, cols = high_ref.shape
+    for half in range(halves):
+        for i in range(rows // edge):
+            for j in range(cols // edge):
+                tile_row = half * (rows // edge) + i
+                tile = total[tile_row * col_tiles + step * (cols // edge) + j]
+                high, low = split(tile)
+                spot = (0, half, pl.ds(i * edge, edge), pl.ds(j * edge, edge))
+                high_ref[spot] = high
+                low_ref[spot] = low
+
+
+def dense_blocks(n_row, n_col, stretch, tile_values, tile_row, tile_col, tile_kind, tile_count):
+    slots, edge, _ = tile_values.shape
+    parts = 8 if slots % 8 == 0 else 1
+    shape = jax.ShapeDtypeStruct((n_row, n_col, stretch, stretch), BF16)
+    block = pl.BlockSpec((1, n_col, stretch, stretch), lambda i: (i, 0, 0, 0))
+    scalars = pl.BlockSpec(memory_space=pltpu.SMEM)
+    tiles = (n_row * stretch // edge) * (n_col * stretch // edge)
+    return pl.pallas_call(
+        dense_kernel,
+        grid=(n_row,),
+        out_shape=(shape, shape),
+        in_specs=[scalars] * 4 + [pl.BlockSpec(memory_space=pl.ANY)],
+        out_specs=(block, block),
+        scratch_shapes=[
+            pltpu.VMEM(tile_values.shape, F32),
+            pltpu.VMEM((tiles, edge, edge), F32),
+            pltpu.SemaphoreType.DMA((parts,)),
+        ],
+        compiler_params=pltpu.CompilerParams(vmem_limit_bytes=48 * 2**20),
+    )(tile_row, tile_col, tile_kind, tile_count, tile_values)
+
+
+def layer_kernel(
+    n_row, n_col, n_rep, features, weight, cotangent, high_hbm, low_hbm,
+    output, input_grad, weight_grad,
+    a_high, a_low, xg, cg, yg, part, part_in, pre, hg, z_own, z_sib, z_far, w_own, w_in, w_all,
+    a_sem, x_send, x_recv, c_send, c_recv, y_send, y_recv, p_send, p_recv, h_send, h_recv,
+    s_send, s_recv, f_send, f_recv, w_send, w_recv, v_send, v_recv,
+):
+    row, col, rep = lax.axis_index("row"), lax.axis_index("col"), lax.axis_index("rep")
+    n_y = n_row // 2
+    core, y = lax.rem(row, 2), lax.div(row, 2)
+    sibling = y * 2 + (1 - core)
+    quarter, stretch = features.shape
+    peers = n_row * n_col
+    me = row * n_col + col
+
+    def peer(k):
+        other = lax.rem(me + k, peers)
+        return other, {"row": lax.div(other, n_col), "col": lax.rem(other, n_col)}
+
+    def far(k):
+        return lax.rem(y + k, n_y)
+
+    def send(src, dst, send_sem, recv_sem, device):
+        return pltpu.make_async_remote_copy(
+            src_ref=src, dst_ref=dst, send_sem=send_sem, recv_sem=recv_sem,
+            device_id=device, device_id_type=MESH,
+        )
+
+    loads = []
+    for k in range(n_row):
+        origin = (row, sibling)[k] if k < 2 else far(k // 2) * 2 + (core, 1 - core)[k % 2]
+        loads.append(origin)
+        pltpu.make_async_copy(high_hbm.at[origin], a_high.at[origin], a_sem.at[0, origin]).start()
+        pltpu.make_async_copy(low_hbm.at[origin], a_low.at[origin], a_sem.at[1, origin]).start()
+
+    barrier = pltpu.get_barrier_semaphore()
+    for k in range(1, peers):
+        pl.semaphore_signal(barrier, inc=1, device_id=peer(k)[1], device_id_type=MESH)
+
+    @pl.when(rep > 0)
+    def _():
+        pl.semaphore_signal(barrier, inc=1, device_id={"rep": rep - 1}, device_id_type=MESH)
+
+    @pl.when(rep < n_rep - 1)
+    def _():
+        pl.semaphore_signal(barrier, inc=1, device_id={"rep": rep + 1}, device_id_type=MESH)
+
+    ends = jnp.where(rep == 0, 1, 0) + jnp.where(rep == n_rep - 1, 1, 0)
+    pl.semaphore_wait(barrier, peers + 1 - ends)
+
+    sent = []
+
+    def start(*args):
+        copy = send(*args)
+        copy.start()
+        sent.append(copy)
+
+    def line_send(buf, send_sem, recv_sem, gap, side, begin):
+        origin = rep - gap * side
+        go = (origin >= 0) & (origin < n_rep) & (rep + side >= 0) & (rep + side < n_rep)
+
+        @pl.when(go)
+        def _():
+            copy = send(
+                buf.at[origin], buf.at[origin], send_sem.at[(side + 1) // 2, gap],
+                recv_sem.at[origin], {"rep": rep + side},
+            )
+            if begin:
+                copy.start()
+            else:
+                copy.wait_send()
+
+    def line_step(buf, send_sem, recv_sem, gap):
+        for side in (1, -1):
+            if gap:
+                origin = rep - gap * side
+
+                @pl.when((origin >= 0) & (origin < n_rep))
+                def _():
+                    send(
+                        buf.at[origin], buf.at[origin], send_sem.at[0, 0],
+                        recv_sem.at[origin], {"rep": rep - side},
+                    ).wait_recv()
+
+            if gap < n_rep - 1:
+                line_send(buf, send_sem, recv_sem, gap, side, True)
+
+    def arrived(buf, recv_sem, device):
+        send(buf, buf, x_send.at[0], recv_sem, device).wait_recv()
+
+    for k in range(1, n_y):
+        start(features, xg.at[row], x_send.at[k], x_recv.at[row], {"row": far(k) * 2 + core})
+    start(features, xg.at[row], x_send.at[0], x_recv.at[row], {"row": sibling})
+    cg[rep] = cotangent[...]
+    line_step(cg, c_send, c_recv, 0)
+    xg[row] = features[...]
+
+    def forward(origin, first, last):
+        for half in (a_high, a_low):
+            which = 0 if half is a_high else 1
+            hbm = (high_hbm, low_hbm)[which]
+            pltpu.make_async_copy(hbm.at[origin], half.at[origin], a_sem.at[which, origin]).wait()
+        high, low = split(xg[origin])
+        stacked = jnp.concatenate([high, low], 0)
+        for k in range(1, n_col + 1):
+            dest = lax.rem(col + k, n_col)
+            term = dot_split(stacked, high, a_high[origin, dest], a_low[origin, dest], NT)
+            part[dest] = term if first else part[dest] + term
+            if last and k < n_col:
+                start(part.at[dest], part_in.at[col], p_send.at[k], p_recv.at[col], {"col": dest})
+
+    forward(row, True, n_row == 1)
+    arrived(xg.at[sibling], x_recv.at[sibling], {"row": sibling})
+    forward(sibling, False, n_row == 2)
+    for k in range(1, n_y):
+        origin = far(k) * 2 + core
+        arrived(xg.at[origin], x_recv.at[origin], {"row": origin})
+        start(
+            xg.at[origin], xg.at[origin], x_send.at[n_y + k - 1], x_recv.at[origin],
+            {"row": sibling},
+        )
+        if k == 1:
+            line_step(cg, c_send, c_recv, 1)
+        forward(origin, False, False)
+        crossed = far(k) * 2 + (1 - core)
+        arrived(xg.at[crossed], x_recv.at[crossed], {"row": sibling})
+        forward(crossed, False, k == n_y - 1)
+    for gap in range(1 if n_y == 1 else 2, n_rep):
+        line_step(cg, c_send, c_recv, gap)
+
+    summed = part[col]
+    for k in range(1, n_col):
+        other = lax.rem(col + k, n_col)
+        arrived(part_in.at[other], p_recv.at[other], {"col": other})
+        summed = summed + part_in[other]
+    yg[rep] = summed
+    line_step(yg, y_send, y_recv, 0)
+    turned = weight[...].T
+    for gap in range(1, n_rep):
+        line_step(yg, y_send, y_recv, gap)
+
+    pre[...] = product(turned, yg[...].reshape(n_rep * quarter, stretch), NN)
+    scale = (2.0 / 3.141592653589793) ** 0.5
+
+    def bend(v):
+        return jnp.tanh(scale * (v + 0.044715 * (v * v * v)))
+
+    v = pre[...]
+    t = bend(v)
+    slope = 0.5 * (1.0 + t) + 0.5 * v * (1.0 - t * t) * (scale * (1.0 + 0.134145 * (v * v)))
+    grad_pre = cg[...].reshape(n_rep * quarter, stretch) * slope
+    g_high, g_low = split(grad_pre)
+    own = weight[pl.ds(pl.multiple_of(rep * quarter, quarter), quarter), :]
+    o_high, o_low = split(own)
+    hg[col] = dot_split(jnp.concatenate([o_high, o_low], 0), o_high, g_high, g_low, NN)
+    for k in range(1, n_col):
+        other = lax.rem(col + k, n_col)
+        start(hg.at[col], hg.at[col], h_send.at[k], h_recv.at[col], {"col": other})
+
+    y_high, y_low = split(yg[rep])
+    w_part = dot_split(jnp.concatenate([y_high, y_low], 0), y_high, g_high, g_low, NT)
+    w_own[...] = w_part.reshape(w_own.shape)
+    for k in range(1, peers):
+        other, device = peer(k)
+        start(w_own.at[other], w_in.at[me], w_send.at[k], w_recv.at[me], device)
+    mine = pre[pl.ds(pl.multiple_of(rep * quarter, quarter), quarter), :]
+    output[...] = 0.5 * mine * (1.0 + bend(mine))
+
+    def back(k, dest):
+        source = lax.rem(col + k, n_col)
+        high, low = split(hg[source])
+        term = dot_split(
+            jnp.concatenate([high, low], 0), high, a_high[dest, source], a_low[dest, source], NN
+        )
+        z_own[dest] = z_own[dest] + term if k else term
+
+    order = [far(k) * 2 + (1 - core) for k in range(1, n_y)] + [sibling]
+    order += [far(k) * 2 + core for k in range(1, n_y)] + [row]
+    for dest in order:
+        back(0, dest)
+    for k in range(1, n_col):
+        other = lax.rem(col + k, n_col)
+        arrived(hg.at[other], h_recv.at[other], {"col": other})
+        for place, dest in enumerate(order):
+            back(k, dest)
+            if k == n_col - 1:
+                ahead = place % n_y + 1
+                spot = far(ahead)
+                if place < n_y:
+                    start(
+                        z_own.at[dest], z_sib.at[spot], s_send.at[place], s_recv.at[spot],
+                        {"row": sibling},
+                    )
+                elif place < n_row - 1:
+                    arrived(z_sib.at[spot], s_recv.at[spot], {"row": sibling})
+                    z_own[dest] = z_own[dest] + z_sib[spot]
+                    start(
+                        z_own.at[dest], z_far.at[y], f_send.at[ahead], f_recv.at[y], {"row": dest}
+                    )
+
+    w_sum = w_own[me]
+    for k in range(1, peers):
+        other, device = peer(k)
+        arrived(w_in.at[other], w_recv.at[other], device)
+        w_sum = w_sum + w_in[other]
+    w_all[me] = w_sum * float(stretch * peers) ** (-0.5)
+    for k in range(1, peers):
+        other, device = peer(k)
+        start(w_all.at[me], w_all.at[me], v_send.at[k], v_recv.at[me], device)
+
+    arrived(z_sib.at[y], s_recv.at[y], {"row": sibling})
+    total = z_own[row] + z_sib[y]
+    for k in range(1, n_y):
+        arrived(z_far.at[far(k)], f_recv.at[far(k)], {"row": far(k) * 2 + core})
+        total = total + z_far[far(k)]
+    input_grad[...] = total
+    for k in range(1, peers):
+        other, device = peer(k)
+        arrived(w_all.at[other], v_recv.at[other], device)
+    weight_grad[...] = w_all[...].reshape(weight_grad.shape)
+
+    for copy in sent:
+        copy.wait_send()
+    for gap in range(n_rep - 1):
+        for side in (1, -1):
+            line_send(cg, c_send, c_recv, gap, side, False)
+            line_send(yg, y_send, y_recv, gap, side, False)
+
+
+def fused(n_row, n_col, n_rep, features, weight, cotangent, tile_values, *slots):
+    quarter, stretch = features.shape
+    width = weight.shape[0]
+    peers = n_row * n_col
+    high, low = dense_blocks(n_row, n_col, stretch, tile_values, *slots)
+    block = (quarter, stretch)
+    vmem = pl.BlockSpec(memory_space=pltpu.VMEM)
+    dma = pltpu.SemaphoreType.DMA
+    piece = (peers, quarter // peers, width)
+    n_y = n_row // 2
+    return pl.pallas_call(
+        functools.partial(layer_kernel, n_row, n_col, n_rep),
+        out_shape=(
+            jax.ShapeDtypeStruct(block, F32),
+            jax.ShapeDtypeStruct(block, F32),
+            jax.ShapeDtypeStruct((quarter, width), F32),
+        ),
+        in_specs=[vmem] * 3 + [pl.BlockSpec(memory_space=pl.ANY)] * 2,
+        out_specs=(vmem,) * 3,
+        scratch_shapes=[
+            pltpu.VMEM(high.shape, BF16),
+            pltpu.VMEM(low.shape, BF16),
+            pltpu.VMEM((n_row, *block), F32),
+            pltpu.VMEM((n_rep, *block), F32),
+            pltpu.VMEM((n_rep, *block), F32),
+            pltpu.VMEM((n_col, *block), F32),
+            pltpu.VMEM((n_col, *block), F32),
+            pltpu.VMEM((n_rep * quarter, stretch), F32),
+            pltpu.VMEM((n_col, *block), F32),
+            pltpu.VMEM((n_row, *block), F32),
+            pltpu.VMEM((n_y, *block), F32),
+            pltpu.VMEM((n_y, *block), F32),
+            pltpu.VMEM(piece, F32),
+            pltpu.VMEM(piece, F32),
+            pltpu.VMEM(piece, F32),
+            dma((2, n_row)),
+            dma((n_row,)), dma((n_row,)),
+            dma((2, n_rep)), dma((n_rep,)),
+            dma((2, n_rep)), dma((n_rep,)),
+            dma((n_col,)), dma((n_col,)),
+            dma((n_col,)), dma((n_col,)),
+            dma((n_y,)), dma((n_y,)),
+            dma((n_y,)), dma((n_y,)),
+            dma((peers,)), dma((peers,)),
+            dma((peers,)), dma((peers,)),
+        ],
+        compiler_params=pltpu.CompilerParams(
+            collective_id=0, has_side_effects=True, vmem_limit_bytes=48 * 2**20
+        ),
+    )(features, weight, cotangent, high, low)
 
 
 def tile_terms(source, values, from_tile, to_tile, tile_kinds, live_weight, dest_tiles, transposed):
@@ -34,10 +408,20 @@
     n_rowdev = lax.axis_size("row")
     n_coldev = lax.axis_size("col")
     n_repdev = lax.axis_size("rep")
-    quarter = weight.shape[0] // n_repdev
-    rep_index = lax.axis_index("rep")
-    own_rows = lax.dynamic_slice_in_dim(weight, rep_index * quarter, quarter, 0)
-    stretch_len = features.shape[1]
+    quarter, stretch_len = features.shape
+    nodes = n_rowdev * n_coldev
+    if (
+        n_rowdev * n_coldev * stretch_len * stretch_len * 4 <= DENSE_BYTES
+        and n_rowdev % 2 == 0
+        and n_coldev > 1
+        and n_repdev > 1
+        and quarter % (8 * nodes) == 0
+    ):
+        return fused(
+            n_rowdev, n_coldev, n_repdev, features, weight, cotangent, tile_values,
+            tile_row, tile_col, tile_kind, tile_count,
+        )
+    own_rows = lax.dynamic_slice_in_dim(weight, lax.axis_index("rep") * quarter, quarter, 0)
     tile_edge = tile_values.shape[1]
     live_count = tile_count[0]
     row_tiles = n_coldev * stretch_len // tile_edge

time: 218 us -> 57.6 us (0.26)
  waiting for transfers between devices: 92.5 us -> 0 us
  matrix products: 53.7 us -> 0 us
  Pallas kernels: 0 us -> 52.1 us
  blocking collectives: 29 us -> 0 us
  local copies, waits for them, and re-layouts: 24.9 us -> 3.98 us
  between operations: 14.5 us -> 1.33 us
  other arithmetic: 2.38 us -> 0 us
    dot_general x7 -> x0, matrix products: 53.7 us -> none  [the longest x1 24.3 us: tile_terms(): jnp.einsum('fgb,gab->fga', picked, chosen, precision=lax.Precision.HIGHEST)]
    psum x1 -> x0, waiting for transfers between devices: 52.3 us -> none  [local(): lax.psum(weight_part * float(node_total) ** (-0.5), ('row', 'col'))]
    pallas_call x0 -> x2, Pallas kernels: none -> 52.1 us  [the longest x1 43.6 us: fused(): pl.pallas_call(functools.partial(layer_kernel, n_row, n_col, n_rep), out_...]
    reduce_scatter x3 -> x0, waiting for transfers between devices: 40.1 us -> none  [the longest x1 21.8 us: local(): lax.psum_scatter(partial_back, 'row', scatter_dimension=1, tiled=True)]
    all_gather x3 -> x0, blocking collectives: 29 us -> none  [the longest x1 15.8 us: local(): whole = lax.all_gather(grad_mixed, 'rep', axis=0, tiled=True)]
    gather x3 -> x0, local copies, waits for them, and re-layouts: 20.7 us -> none  [the longest x1 14.2 us: tile_terms(): chosen = jnp.take(values, tile_kinds, axis=0)]
  transfers between devices with their start and end apart: 4 -> 0, of which waited for: 4 -> 0; matrix products, arithmetic and copies ran while one was open for 7% -> 0% of each run, Pallas kernels for 0% -> 0%
where the time goes in v1:
time: 57.6 us; the launch traced here: 57.4 us
  Pallas kernels  52.1 us (90%)
  local copies, waits for them, and re-layouts  3.98 us (7%)
  between operations  1.33 us (2%)
    pallas_call x1, Pallas kernels, fused(): pl.pallas_call(functools.partial(layer_kernel, n_row, n_col, n_rep), out_...  43.6 us
    pallas_call x1, Pallas kernels, dense_blocks(): pl.pallas_call(dense_kernel, grid=(n_row,), out_shape=(shape, shape), in_...  8.54 us
    unnamed x15, local copies, waits for them, and re-layouts  3.98 us

profile of v1, /device:TPU:0, one launch (start us, length us, event | category | flops | bytes accessed | tf_op | source)
XLA Modules:
  0.0 57.4 jit_solution(9280926829366432939)
XLA Ops:
  1.3 0.0 copy-start.3
  1.3 0.7 %copy-done.3 = s32[160]{0:T(256)S(1)} copy-done((s32[160]{0:T(256)S(1)}, s32[160]{0:T(256)}, u32[]{:S(2)}) %copy-start.3) | copy-done | bytes 664
  2.0 0.0 copy-start.4
  2.0 0.7 %copy-done.4 = s32[160]{0:T(256)S(1)} copy-done((s32[160]{0:T(256)S(1)}, s32[160]{0:T(256)}, u32[]{:S(2)}) %copy-start.4) | copy-done | bytes 664
  2.6 0.0 copy-start.5
  2.6 0.7 %copy-done.5 = s32[160]{0:T(256)S(1)} copy-done((s32[160]{0:T(256)S(1)}, s32[160]{0:T(256)}, u32[]{:S(2)}) %copy-start.5) | copy-done | bytes 664
  3.3 0.0 copy-start
  3.3 0.0 copy-start.1
  3.3 0.0 copy-start.2
  3.3 8.5 %shard_map.103 = (bf16[4,2,512,512]{3,2,1,0:T(8,128)(2,1)S(1)}, bf16[4,2,512,512]{3,2,1,0:T(8,128)(2,1)}) custom-call(s32[160]{0:T(256)S(1)} %copy-done.3, s32[160]{0:T(256)S(1)} %copy-done.4, s32[160]{0:T(256)S(1)} %copy-done.5, s32[1]{0:T(128)S(6)} %copy.14.count_ref, f32[160,128,128]{2,1,0:T(8,128)} %values.1), custom_call_target="tpu_custom_call" | custom-call | tf_op jit(solution)/shard_map/pallas_call | solution.py:85
  11.9 0.0 copy-done
  11.9 0.0 copy-done.1
  11.9 0.0 copy-done.2
  11.9 43.6 %shard_map.104 = (f32[64,512]{1,0:T(8,128)S(1)}, f32[64,512]{1,0:T(8,128)S(1)}, f32[64,256]{1,0:T(8,128)S(1)}) custom-call(f32[64,512]{1,0:T(8,128)S(1)} %copy-done.1, f32[256,256]{1,0:T(8,128)S(1)} %copy-done, f32[64,512]{1,0:T(8,128)S(1)} %copy-done.2, bf16[4,2,512,512]{3,2,1,0:T(8,128)(2,1)S(1)} %get-tuple-element.5.high_hbm, ...), custom_call_target="tpu_custom_call" | custom-call | tf_op jit(solution)/shard_map/pallas_call | solution.py:339
  55.5 0.7 %copy.15 = f32[64,512]{1,0:T(8,128)} copy(f32[64,512]{1,0:T(8,128)S(1)} %get-tuple-element.10) | data formatting | bytes 262144
  56.2 0.7 %copy.16 = f32[64,512]{1,0:T(8,128)} copy(f32[64,512]{1,0:T(8,128)S(1)} %get-tuple-element.11) | data formatting | bytes 262144
  56.8 0.6 %copy.17 = f32[64,256]{1,0:T(8,128)} copy(f32[64,256]{1,0:T(8,128)S(1)} %get-tuple-element.12) | data formatting | bytes 131072
Async XLA Ops:
  1.3 0.7 %copy-start.3 = (s32[160]{0:T(256)S(1)}, s32[160]{0:T(256)}, u32[]{:S(2)}) copy-start(s32[160]{0:T(256)} %row_ref.1) | copy-start | bytes 1924
  2.0 0.7 %copy-start.4 = (s32[160]{0:T(256)S(1)}, s32[160]{0:T(256)}, u32[]{:S(2)}) copy-start(s32[160]{0:T(256)} %col_ref.1) | copy-start | bytes 1924
  2.6 0.7 %copy-start.5 = (s32[160]{0:T(256)S(1)}, s32[160]{0:T(256)}, u32[]{:S(2)}) copy-start(s32[160]{0:T(256)} %kind_ref.1) | copy-start | bytes 1924
  3.3 8.6 %copy-start = (f32[256,256]{1,0:T(8,128)S(1)}, f32[256,256]{1,0:T(8,128)}, u32[]{:S(2)}) copy-start(f32[256,256]{1,0:T(8,128)} %weight.1) | copy-start | bytes 786436
  3.3 8.6 %copy-start.1 = (f32[64,512]{1,0:T(8,128)S(1)}, f32[64,512]{1,0:T(8,128)}, u32[]{:S(2)}) copy-start(f32[64,512]{1,0:T(8,128)} %features.1) | copy-start | bytes 393220
  3.3 8.6 %copy-start.2 = (f32[64,512]{1,0:T(8,128)S(1)}, f32[64,512]{1,0:T(8,128)}, u32[]{:S(2)}) copy-start(f32[64,512]{1,0:T(8,128)} %cotangent.1) | copy-start | bytes 393220

commit v2 on v1

--- a/solution.py
+++ b/solution.py
@@ -31,84 +31,38 @@
     return dot_split(jnp.concatenate([a_high, a_low], 0), a_high, *split(b), dims)
 
 
-def dense_kernel(row_ref, col_ref, kind_ref, count_ref, values, high_ref, low_ref, held, total, sems):
-    step = pl.program_id(0)
-    edge = held.shape[1]
-    col_tiles = pl.num_programs(0) * (high_ref.shape[3] // edge)
-
-    @pl.when(step == 0)
-    def _():
-        parts = sems.shape[0]
-        size = held.shape[0] // parts
-        copies = [
-            pltpu.make_async_copy(
-                values.at[pl.ds(k * size, size)], held.at[pl.ds(k * size, size)], sems.at[k]
-            )
-            for k in range(parts)
-        ]
-        for copy in copies:
-            copy.start()
-
-        @pl.loop(0, total.shape[0])
-        def _(place):
-            total[place] = jnp.zeros(total.shape[1:], F32)
-
-        for copy in copies:
-            copy.wait()
-
-        def add(slot, carry):
-            place = row_ref[slot] * col_tiles + col_ref[slot]
-            total[place] = total[place] + held[kind_ref[slot]]
-            return carry
-
-        lax.fori_loop(0, count_ref[0], add, 0)
-
-    _, halves, rows, cols = high_ref.shape
-    for half in range(halves):
-        for i in range(rows // edge):
-            for j in range(cols // edge):
-                tile_row = half * (rows // edge) + i
-                tile = total[tile_row * col_tiles + step * (cols // edge) + j]
-                high, low = split(tile)
-                spot = (0, half, pl.ds(i * edge, edge), pl.ds(j * edge, edge))
-                high_ref[spot] = high
-                low_ref[spot] = low
-
-
-def dense_blocks(n_row, n_col, stretch, tile_values, tile_row, tile_col, tile_kind, tile_count):
-    slots, edge, _ = tile_values.shape
-    parts = 8 if slots % 8 == 0 else 1
-    shape = jax.ShapeDtypeStruct((n_row, n_col, stretch, stretch), BF16)
-    block = pl.BlockSpec((1, n_col, stretch, stretch), lambda i: (i, 0, 0, 0))
-    scalars = pl.BlockSpec(memory_space=pltpu.SMEM)
-    tiles = (n_row * stretch // edge) * (n_col * stretch // edge)
-    return pl.pallas_call(
-        dense_kernel,
-        grid=(n_row,),
-        out_shape=(shape, shape),
-        in_specs=[scalars] * 4 + [pl.BlockSpec(memory_space=pl.ANY)],
-        out_specs=(block, block),
-        scratch_shapes=[
-            pltpu.VMEM(tile_values.shape, F32),
-            pltpu.VMEM((tiles, edge, edge), F32),
-            pltpu.SemaphoreType.DMA((parts,)),
-        ],
-        compiler_params=pltpu.CompilerParams(vmem_limit_bytes=48 * 2**20),
-    )(tile_row, tile_col, tile_kind, tile_count, tile_values)
+def chain_links(row_tiles, col_tiles, count, tile_row, tile_col):
+    slots = tile_row.shape[1]
+    queries = slots + row_tiles * col_tiles
+    place = tile_row * col_tiles + tile_col
+    shape = (slots, slots)
+    key, query = (lax.broadcasted_iota(jnp.int32, shape, axis) for axis in (0, 1))
+    keys = jnp.max(jnp.where(key == query, place, 0), axis=1, keepdims=True)
+
+    def latest(hit, key):
+        last = jnp.max(jnp.where(hit & (key < count), key, -1), axis=0, keepdims=True)
+        return jnp.where(last < 0, slots, last)
+
+    before = latest((keys == place) & (key < query), key)
+    shape = (slots, row_tiles * col_tiles)
+    key, query = (lax.broadcasted_iota(jnp.int32, shape, axis) for axis in (0, 1))
+    return before, latest(keys == query, key)
 
 
 def layer_kernel(
-    n_row, n_col, n_rep, features, weight, cotangent, high_hbm, low_hbm,
+    n_row, n_col, n_rep, kind, count, tile_row, tile_col, features_in, weight_in, cotangent_in, values_in,
     output, input_grad, weight_grad,
-    a_high, a_low, xg, cg, yg, part, part_in, pre, hg, z_own, z_sib, z_far, w_own, w_in, w_all,
-    a_sem, x_send, x_recv, c_send, c_recv, y_send, y_recv, p_send, p_recv, h_send, h_recv,
+    before_v, last_v, before, last, held, chain, weight, a_high, a_low, xs, xg, cg, yg, part, part_in, pre, hg, z_own, z_sib, z_far, w_own, w_in, w_all,
+    l_sem, i_sem, t_sem, x_send, x_recv, c_send, c_recv, y_send, y_recv, p_send, p_recv, h_send, h_recv,
     s_send, s_recv, f_send, f_recv, w_send, w_recv, v_send, v_recv,
 ):
     row, col, rep = lax.axis_index("row"), lax.axis_index("col"), lax.axis_index("rep")
     n_y = n_row // 2
     core, y = lax.rem(row, 2), lax.div(row, 2)
     sibling = y * 2 + (1 - core)
-    quarter, stretch = features.shape
+    quarter, stretch = features_in.shape
+    slots, edge, _ = held.shape
+    tiles = stretch // edge
     peers = n_row * n_col
     me = row * n_col + col
 
@@ -125,12 +79,30 @@
             device_id=device, device_id_type=MESH,
         )
 
-    loads = []
-    for k in range(n_row):
-        origin = (row, sibling)[k] if k < 2 else far(k // 2) * 2 + (core, 1 - core)[k % 2]
-        loads.append(origin)
-        pltpu.make_async_copy(high_hbm.at[origin], a_high.at[origin], a_sem.at[0, origin]).start()
-        pltpu.make_async_copy(low_hbm.at[origin], a_low.at[origin], a_sem.at[1, origin]).start()
+    inputs = [
+        pltpu.make_async_copy(features_in, xg.at[row], i_sem.at[0]),
+        pltpu.make_async_copy(cotangent_in, cg.at[rep], i_sem.at[1]),
+        pltpu.make_async_copy(weight_in, weight, i_sem.at[2]),
+    ]
+    parts = t_sem.shape[0]
+    size = slots // parts
+    for k in range(parts):
+        piece = pl.ds(k * size, size)
+        inputs.append(pltpu.make_async_copy(values_in.at[piece], held.at[piece], t_sem.at[k]))
+    for copy in inputs:
+        copy.start()
+
+    links = chain_links(
+        n_col * tiles, n_row * tiles, count[0],
+        tile_row[...].reshape(1, slots), tile_col[...].reshape(1, slots),
+    )
+    before_v[...], last_v[...] = links
+    moves = [
+        pltpu.make_async_copy(before_v, before, l_sem.at[0]),
+        pltpu.make_async_copy(last_v, last, l_sem.at[1]),
+    ]
+    for copy in moves:
+        copy.start()
 
     barrier = pltpu.get_barrier_semaphore()
     for k in range(1, peers):
@@ -187,30 +159,27 @@
     def arrived(buf, recv_sem, device):
         send(buf, buf, x_send.at[0], recv_sem, device).wait_recv()
 
+    inputs[0].wait()
     for k in range(1, n_y):
-        start(features, xg.at[row], x_send.at[k], x_recv.at[row], {"row": far(k) * 2 + core})
-    start(features, xg.at[row], x_send.at[0], x_recv.at[row], {"row": sibling})
-    cg[rep] = cotangent[...]
+        start(xg.at[row], xg.at[row], x_send.at[k], x_recv.at[row], {"row": far(k) * 2 + core})
+    start(xg.at[row], xg.at[row], x_send.at[0], x_recv.at[row], {"row": sibling})
+    inputs[1].wait()
     line_step(cg, c_send, c_recv, 0)
-    xg[row] = features[...]
-
-    def forward(origin, first, last):
-        for half in (a_high, a_low):
-            which = 0 if half is a_high else 1
-            hbm = (high_hbm, low_hbm)[which]
-            pltpu.make_async_copy(hbm.at[origin], half.at[origin], a_sem.at[which, origin]).wait()
+
+    for copy in inputs[2:] + moves:
+        copy.wait()
+    chain[slots] = jnp.zeros((edge, edge), F32)
+
+    @pl.loop(0, slots, unroll=4 if slots % 4 == 0 else 1)
+    def _(slot):
+        chain[slot] = held[kind[slot]] + chain[before[0, slot]]
+
+    def ready(origin):
         high, low = split(xg[origin])
-        stacked = jnp.concatenate([high, low], 0)
-        for k in range(1, n_col + 1):
-            dest = lax.rem(col + k, n_col)
-            term = dot_split(stacked, high, a_high[origin, dest], a_low[origin, dest], NT)
-            part[dest] = term if first else part[dest] + term
-            if last and k < n_col:
-                start(part.at[dest], part_in.at[col], p_send.at[k], p_recv.at[col], {"col": dest})
-
-    forward(row, True, n_row == 1)
-    arrived(xg.at[sibling], x_recv.at[sibling], {"row": sibling})
-    forward(sibling, False, n_row == 2)
+        xs[origin, :quarter, :] = high
+        xs[origin, quarter:, :] = low
+
+    ready(row)
     for k in range(1, n_y):
         origin = far(k) * 2 + core
         arrived(xg.at[origin], x_recv.at[origin], {"row": origin})
@@ -218,14 +187,42 @@
             xg.at[origin], xg.at[origin], x_send.at[n_y + k - 1], x_recv.at[origin],
             {"row": sibling},
         )
+        ready(origin)
+    arrived(xg.at[sibling], x_recv.at[sibling], {"row": sibling})
+    ready(sibling)
+    line_step(cg, c_send, c_recv, 1)
+
+    def dense(origin, dest):
+        @pl.loop(0, tiles)
+        def _(i):
+            for j in range(tiles):
+                place = ((dest * tiles + i) * n_row + origin) * tiles + j
+                high, low = split(chain[last[0, place]])
+                rows = pl.ds(pl.multiple_of(i * edge, edge), edge)
+                a_high[origin, dest, rows, pl.ds(j * edge, edge)] = high
+                a_low[origin, dest, rows, pl.ds(j * edge, edge)] = low
+
+    for k in range(1, n_col + 1):
+        dest = lax.rem(col + k, n_col)
+        for place in range(n_row):
+            if place < n_y:
+                origin = far(place) * 2 + core
+            else:
+                origin = far(place - n_y) * 2 + (1 - core)
+            if k == 1 and place > n_y:
+                arrived(xg.at[origin], x_recv.at[origin], {"row": sibling})
+                ready(origin)
+            dense(origin, dest)
+            stacked = xs[origin]
+            term = dot_split(
+                stacked, stacked[:quarter], a_high[origin, dest], a_low[origin, dest], NT
+            )
+            part[dest] = part[dest] + term if place else term
+        if k < n_col:
+            start(part.at[dest], part_in.at[col], p_send.at[k], p_recv.at[col], {"col": dest})
         if k == 1:
-            line_step(cg, c_send, c_recv, 1)
-        forward(origin, False, False)
-        crossed = far(k) * 2 + (1 - core)
-        arrived(xg.at[crossed], x_recv.at[crossed], {"row": sibling})
-        forward(crossed, False, k == n_y - 1)
-    for gap in range(1 if n_y == 1 else 2, n_rep):
-        line_step(cg, c_send, c_recv, gap)
+            for gap in range(2, n_rep):
+                line_step(cg, c_send, c_recv, gap)
 
     summed = part[col]
     for k in range(1, n_col):
@@ -326,13 +323,20 @@
             line_send(yg, y_send, y_recv, gap, side, False)
 
 
-def fused(n_row, n_col, n_rep, features, weight, cotangent, tile_values, *slots):
+def fused(
+    n_row, n_col, n_rep, features, weight, cotangent, tile_values, tile_row, tile_col, tile_kind,
+    tile_count,
+):
     quarter, stretch = features.shape
     width = weight.shape[0]
     peers = n_row * n_col
-    high, low = dense_blocks(n_row, n_col, stretch, tile_values, *slots)
+    slots, edge, _ = tile_values.shape
+    row_tiles, col_tiles = n_col * stretch // edge, n_row * stretch // edge
+    parts = 8 if slots % 8 == 0 else 1
+    dense = (n_row, n_col, stretch, stretch)
     block = (quarter, stretch)
     vmem = pl.BlockSpec(memory_space=pltpu.VMEM)
+    smem = pl.BlockSpec(memory_space=pltpu.SMEM)
     dma = pltpu.SemaphoreType.DMA
     piece = (peers, quarter // peers, width)
     n_y = n_row // 2
@@ -343,11 +347,19 @@
             jax.ShapeDtypeStruct(block, F32),
             jax.ShapeDtypeStruct((quarter, width), F32),
         ),
-        in_specs=[vmem] * 3 + [pl.BlockSpec(memory_space=pl.ANY)] * 2,
+        in_specs=[smem] * 2 + [vmem] * 2 + [pl.BlockSpec(memory_space=pl.ANY)] * 4,
         out_specs=(vmem,) * 3,
         scratch_shapes=[
-            pltpu.VMEM(high.shape, BF16),
-            pltpu.VMEM(low.shape, BF16),
+            pltpu.VMEM((1, slots), jnp.int32),
+            pltpu.VMEM((1, row_tiles * col_tiles), jnp.int32),
+            pltpu.SMEM((1, slots), jnp.int32),
+            pltpu.SMEM((1, row_tiles * col_tiles), jnp.int32),
+            pltpu.VMEM(tile_values.shape, F32),
+            pltpu.VMEM((slots + 1, edge, edge), F32),
+            pltpu.VMEM(weight.shape, F32),
+            pltpu.VMEM(dense, BF16),
+            pltpu.VMEM(dense, BF16),
+            pltpu.VMEM((n_row, 2 * quarter, stretch), BF16),
             pltpu.VMEM((n_row, *block), F32),
             pltpu.VMEM((n_rep, *block), F32),
             pltpu.VMEM((n_rep, *block), F32),
@@ -361,7 +373,7 @@
             pltpu.VMEM(piece, F32),
             pltpu.VMEM(piece, F32),
             pltpu.VMEM(piece, F32),
-            dma((2, n_row)),
+            dma((2,)), dma((3,)), dma((parts,)),
             dma((n_row,)), dma((n_row,)),
             dma((2, n_rep)), dma((n_rep,)),
             dma((2, n_rep)), dma((n_rep,)),
@@ -373,9 +385,9 @@
             dma((peers,)), dma((peers,)),
         ],
         compiler_params=pltpu.CompilerParams(
-            collective_id=0, has_side_effects=True, vmem_limit_bytes=48 * 2**20
+            collective_id=0, has_side_effects=True, vmem_limit_bytes=56 * 2**20
         ),
-    )(features, weight, cotangent, high, low)
+    )(tile_kind, tile_count, tile_row, tile_col, features, weight, cotangent, tile_values)
 
 
 def tile_terms(source, values, from_tile, to_tile, tile_kinds, live_weight, dest_tiles, transposed):
@@ -416,6 +428,7 @@
         and n_coldev > 1
         and n_repdev > 1
         and quarter % (8 * nodes) == 0
+        and tile_values.size * 4 <= DENSE_BYTES
     ):
         return fused(
             n_rowdev, n_coldev, n_repdev, features, weight, cotangent, tile_values,

time: 57.6 us -> 52.9 us (0.918)
  Pallas kernels: 52.1 us -> 46.7 us
  local copies, waits for them, and re-layouts: 3.98 us -> 4.61 us
    pallas_call x1 -> x0, Pallas kernels: 8.54 us -> none  [dense_blocks(): pl.pallas_call(dense_kernel, grid=(n_row,), out_shape=(shape, shape), in_...]
    pallas_call x1, Pallas kernels: 43.6 us -> 46.7 us  [fused(): pl.pallas_call(functools.partial(layer_kernel, n_row, n_col, n_rep), out_...]
    unnamed x15 -> x3, local copies, waits for them, and re-layouts: 3.98 us -> 4.61 us
where the time goes in v2:
time: 52.9 us; the launch traced here: 52.6 us
  Pallas kernels  46.7 us (88%)
  local copies, waits for them, and re-layouts  4.61 us (9%)
  between operations  1.29 us (2%)
    pallas_call x1, Pallas kernels, fused(): pl.pallas_call(functools.partial(layer_kernel, n_row, n_col, n_rep), out_...  46.7 us
    unnamed x3, local copies, waits for them, and re-layouts  4.61 us

profile of v2, /device:TPU:0, one launch (start us, length us, event | category | flops | bytes accessed | tf_op | source)
XLA Modules:
  0.0 52.6 jit_solution(11676806868558652513)
XLA Ops:
  1.3 46.7 %shard_map.103 = (f32[64,512]{1,0:T(8,128)}, f32[64,512]{1,0:T(8,128)}, f32[64,256]{1,0:T(8,128)}) custom-call(s32[160]{0:T(256)} %kind.1, s32[1]{0:T(128)S(6)} %copy.14.count, s32[160]{0:T(256)} %tile_row.1, s32[160]{0:T(256)} %tile_col.1, f32[64,512]{1,0:T(8,128)} %features_in.1, f32[256,256]{1,0:T(8,128)} %weight_in.1, f32[64,512]{1,0:T(8,128)} %cotangent_in.1, ...), custom_call_target="tpu_custom_call" | custom-call | tf_op jit(solution)/shard_map/pallas_call | solution.py:343
  48.0 1.6 %copy.15 = f32[64,512]{1,0:T(8,128)} copy(f32[64,512]{1,0:T(8,128)} %get-tuple-element.6) | data formatting | bytes 262144
  49.6 1.6 %copy.16 = f32[64,512]{1,0:T(8,128)} copy(f32[64,512]{1,0:T(8,128)} %get-tuple-element.7) | data formatting | bytes 262144
  51.2 1.5 %copy.17 = f32[64,256]{1,0:T(8,128)} copy(f32[64,256]{1,0:T(8,128)} %get-tuple-element.8) | data formatting | bytes 131072
